TPU v7x, 32 devices: a whole 2x2x4 slice. The times are simulated.
32 devices in a mesh: seq: 8 (over z, y), head: 4 (over x, core).
Axes of the slice: x: 2, y: 2, z: 4, core: 2. Of those that a mesh axis runs over, the one named last changes fastest.
Arguments:
- queries: bfloat16 [1024, 2048], P('seq', 'head'), may hold values from -6 to 6
- vision: bfloat16 [1600, 8192], P('seq'), may hold values from -6 to 6
- kv_weight: bfloat16 [2, 8192, 256], P(None, None, 'head'), may hold values from -0.75 to 0.75
- out_weight: bfloat16 [2048, 8192], P('head', 'seq'), may hold values from -0.1875 to 0.1875
- q_gain: float32 [128], replicated, may hold values from 0.1 to 1.9
- k_gain: float32 [128], replicated, may hold values from 0.1 to 1.9
- tile_counts: int32 [4], replicated, may hold values from 200 to 400, as said below
- spans: int32 [1024, 2], P('seq'), may hold values from 0 to 4, as said below
Outputs:
- output: bfloat16 [1024, 8192], P('seq', 'head')
Inputs may be any that keep to these rules, and one draw needn't show every extreme that they name: `tile_counts`: every tile holds at least 200 vision tokens in its first slots; one tile is full with exactly 400. For every token spans[t, 0] < spans[t, 1], so each token attends one or more whole tiles.
All inputs are finite; a program needn't handle non-finite values.
Results may differ from a plain program's by a relative error of at most 0.0085.
Values may be sent and summed in bfloat16 or wider, within the bound.
A program may use at most 64 MiB of HBM per device.

v0:
```python
import math

import jax
import jax.numpy as jnp
from jax import lax
from jax.sharding import PartitionSpec as P

HD = 128
TILES = 4


EPSILON = 1e-05


def swapped(value, axis, apart):
    mask = 2**apart
    pairs = [(source, source ^ mask) for source in range(lax.axis_size(axis))]
    return lax.ppermute(value, axis, pairs)


def rms_scale(field, gain):
    mean_sq = jnp.mean(field * field, axis=-1, keepdims=True)
    return field / jnp.sqrt(mean_sq + EPSILON) * gain


def local(queries, vision, kv_weight, out_weight, q_gain, k_gain, tile_counts, spans):
    row_count = queries.shape[0]
    heads_here = queries.shape[1] // HD
    half_cols = kv_weight.shape[2]
    vis_local = vision.shape[0]
    slot_cap = vis_local * lax.axis_size("seq") // TILES
    factor = 1.0 / math.sqrt(HD)
    query_f = queries.astype(jnp.float32).reshape(row_count, heads_here, HD)
    q_normed = rms_scale(query_f, q_gain).astype(jnp.bfloat16)
    both_weights = jnp.concatenate([kv_weight[0], kv_weight[1]], axis=1)
    projected = jnp.dot(vision, both_weights, preferred_element_type=jnp.float32)
    key_raw = projected[:, :half_cols]
    value_half = projected[:, half_cols:].astype(jnp.bfloat16)
    own_squares = jnp.sum(key_raw * key_raw, axis=1)
    other_squares = swapped(own_squares, "head", 0)
    inverse = 1.0 / jnp.sqrt((own_squares + other_squares) / HD + EPSILON)
    parity = lax.axis_index("head") % 2
    gain_half = lax.dynamic_slice_in_dim(k_gain, parity * half_cols, half_cols)
    key_half = (key_raw * inverse[:, None] * gain_half[None, :]).astype(jnp.bfloat16)
    local_pair = jnp.concatenate([key_half, value_half], axis=1)
    first_tile = spans[:, 0]
    end_tile = spans[:, 1]
    tile_ids = jnp.arange(TILES, dtype=jnp.int32)
    numer = jnp.zeros((row_count, heads_here, HD), jnp.float32)
    totals = jnp.zeros((heads_here, row_count), jnp.float32)
    gathered = lax.all_gather(local_pair, "seq", axis=0, tiled=True)
    partner = swapped(gathered, "head", 0)
    lower_half = jnp.where(parity == 0, gathered, partner)
    upper_half = jnp.where(parity == 0, partner, gathered)
    assemble_key_block = jnp.concatenate(
        [lower_half[:, :half_cols], upper_half[:, :half_cols]], axis=1
    )
    assemble_value_block = jnp.concatenate(
        [lower_half[:, half_cols:], upper_half[:, half_cols:]], axis=1
    )
    for tile_index in range(TILES):
        key_block = assemble_key_block[tile_index * slot_cap : (tile_index + 1) * slot_cap]
        value_block = assemble_value_block[tile_index * slot_cap : (tile_index + 1) * slot_cap]
        key_index = tile_index * slot_cap + jnp.arange(key_block.shape[0], dtype=jnp.int32)
        tile_of = key_index // slot_cap
        slot_of = key_index % slot_cap
        count_of = jnp.sum(
            jnp.where(tile_of[:, None] == tile_ids[None, :], tile_counts[None, :], 0), axis=1
        )
        allowed = (
            (slot_of < count_of)[None, :]
            & (first_tile[:, None] <= tile_of[None, :])
            & (tile_of[None, :] < end_tile[:, None])
        )
        scores = (
            jnp.einsum("rhd,nd->hrn", q_normed, key_block, preferred_element_type=jnp.float32)
            * factor
        )
        weights = jnp.where(allowed[None, :, :], jnp.exp(scores), jnp.zeros_like(scores))
        total_part = jnp.sum(weights, axis=2)
        numer_part = jnp.einsum(
            "hrn,nd->rhd",
            weights.astype(jnp.bfloat16),
            value_block,
            preferred_element_type=jnp.float32,
        )
        numer_part, total_part = (numer_part, total_part)
        numer = numer + numer_part
        totals = totals + total_part
    attended = (
        (numer / jnp.transpose(totals)[:, :, None])
        .astype(jnp.bfloat16)
        .reshape(row_count, heads_here * HD)
    )
    partial_value = jnp.dot(
        attended,
        lax.all_gather(out_weight, "seq", axis=1, tiled=True),
        preferred_element_type=jnp.float32,
    )
    return lax.psum_scatter(partial_value, "head", scatter_dimension=1, tiled=True).astype(
        jnp.bfloat16
    )


def solution(mesh):
    return jax.shard_map(
        local,
        mesh=mesh,
        in_specs=(
            P("seq", "head"),
            P("seq", None),
            P(None, None, "head"),
            P("head", "seq"),
            P(),
            P(),
            P(),
            P("seq", None),
        ),
        out_specs=P("seq", "head"),
        check_vma=False,
    )
```

profile of v0, /device:TPU:3, one launch (start us, length us, event | category | flops | bytes accessed | tf_op | source)
XLA Modules:
  0.0 196.6 jit_solution(4449070792973059252)
XLA Ops:
  6.5 0.0 copy-start
  6.5 0.0 all-gather.2.cloned.1.call-start
  6.5 0.7 all-gather.2.cloned.1.call-update
  7.3 0.0 reduce-scatter.2.cloned.1.call-start
  7.3 1.9 slice_bitcast_fusion.1
  9.2 0.0 copy-done
  9.2 0.0 copy-start.7
  9.2 0.0 copy-start.5
  9.2 0.0 copy-start.8
  9.2 0.0 copy-start.6
  9.3 1.1 fusion.19
  10.4 0.1 multiply_reduce_fusion.1
  10.5 0.7 collective-permute-start
  11.2 1.0 copy.20
  12.3 0.0 copy-done.7
  12.3 0.1 select_reduce_fusion
  12.4 0.0 copy-done.5
  12.5 1.3 compare_and_fusion
  13.8 0.7 slice.158
  14.5 0.8 copy.23
  15.3 0.0 copy-done.8
  15.3 0.1 dynamic_slice.3
  15.4 0.0 collective-permute-done
  15.4 0.1 multiply_convert_fusion.1
  15.5 0.9 pad_maximum_fusion.2
  16.4 27.0 %all_gather.6 = bf16[1600,128]{1,0:T(8,128)(2,1)S(1)} all-gather(bf16[200,128]{1,0:T(8,128)(2,1)S(1)} %pad_maximum_fusion.2), channel_id=1, replica_groups=mesh['seq'=8,'head'=4] {'seq'}, dimensions={0}, use_global_device_ids=true | all-gather | bytes 460800 | tf_op jit(solution)/shard_map/all_gather | solution.py:51
  43.4 5.7 %collective-permute-start.1 = (bf16[1600,128]{1,0:T(8,128)(2,1)S(1)}, bf16[1600,128]{1,0:T(8,128)(2,1)S(1)}, u32[]{:S(2)}, u32[]{:S(2)}) collective-permute-start(bf16[1600,128]{1,0:T(8,128)(2,1)S(1)} %all_gather.6), channel_id=1, source_target_pairs={{0,1},{1,0},{2,3},{3,2},{4,5},{5,4},{6,7},{7,6},{8,9},{9,8},{10,11... | collective-permute-start | bytes 1228808 | tf_op jit(solution)/shard_map/ppermute | solution.py:18
  49.1 0.0 copy-done.6
  49.1 1.1 multiply_convert_fusion
  50.2 0.0 copy-start.3
  50.3 0.3 collective-permute-done.1
  50.5 0.1 broadcast_select_fusion
  50.6 0.0 copy-start.1
  50.6 0.0 copy-start.2
  50.6 0.3 fusion.75
  50.9 0.4 fusion.79
  51.3 0.4 fusion.80
  51.7 0.4 fusion.77
  52.2 0.4 fusion.78
  52.6 0.3 fusion.25
  52.9 0.3 convolution_add_fusion.2
  53.2 0.3 convolution_add_fusion.1
  53.6 0.3 fusion.18
  53.9 84.8 %all-gather.2.cloned.1.call-done = bf16[512,8192]{1,0:T(8,128)(2,1)} async-done(((bf16[512,1024]{1,0:T(8,128)(2,1)}), bf16[512,8192]{1,0:T(8,128)(2,1)}) %all-gather.2.cloned.1.call-update) | async-done | bytes 8388624 | tf_op jit(solution)/shard_map/all_gather | solution.py:97
  138.7 6.7 %fusion.81 = f32[128,8192]{1,0:T(8,128)} fusion(bf16[128,512]{0,1:T(8,128)(2,1)S(1)} %bitcast.82, bf16[512,8192]{1,0:T(8,128)(2,1)} %all-gather.2.cloned.1.call-done), kind=kOutput, calls=%fused_computation.136 | convolution fusion | flops 1073741824 | bytes 12713984 | tf_op jit(solution)/shard_map/dot_general | solution.py:95
  145.4 0.0 reduce-scatter.2.cloned.1.call-update
  145.4 42.3 %reduce-scatter.2.cloned.1.call-done = f32[128,2048]{1,0:T(8,128)} async-done(((f32[128,8192]{1,0:T(8,128)}), f32[128,2048]{1,0:T(8,128)}) %reduce-scatter.2.cloned.1.call-update) | async-done | bytes 1048592 | tf_op jit(solution)/shard_map/reduce_scatter | solution.py:100
  187.7 2.1 %convert_element_type.33 = bf16[128,2048]{1,0:T(8,128)(2,1)} convert(f32[128,2048]{1,0:T(8,128)} %reduce-scatter.2.cloned.1.call-done) | non-fusion elementwise | flops 262144 | bytes 1572864 | tf_op jit(solution)/shard_map/convert_element_type | solution.py:100
  (16 shorter events, 0.1 us)
Async XLA Ops:
  6.5 2.7 %copy-start = (bf16[200,8192]{1,0:T(8,128)(2,1)S(1)}, bf16[200,8192]{1,0:T(8,128)(2,1)}, u32[]{:S(2)}) copy-start(bf16[200,8192]{1,0:T(8,128)(2,1)} %param.9) | copy-start | bytes 9830404
  6.5 132.2 %all-gather.2.cloned.1.call-start = ((), (), s32[]{:S(2)}) async-start(), calls=%async_computation.1 | async-start | bytes 9437184 | tf_op jit(solution)/shard_map/all_gather | solution.py:97
  7.3 180.4 %reduce-scatter.2.cloned.1.call-start = ((), (), s32[]{:S(2)}) async-start(), calls=%async_computation.2 | async-start | bytes 5242880 | tf_op jit(solution)/shard_map/reduce_scatter | solution.py:100
  9.2 3.1 %copy-start.7 = (s32[4]{0:T(128)S(1)}, s32[4]{0:T(128)}, u32[]{:S(2)}) copy-start(s32[4]{0:T(128)} %param.14) | copy-start | bytes 52
  9.2 3.2 %copy-start.5 = (s32[128,2]{0,1:T(2,128)S(1)}, s32[128,2]{0,1:T(2,128)}, u32[]{:S(2)}) copy-start(s32[128,2]{0,1:T(2,128)} %param.15) | copy-start | bytes 3076
  9.2 6.1 %copy-start.8 = (f32[128]{0:T(128)S(1)}, f32[128]{0:T(128)}, u32[]{:S(2)}) copy-start(f32[128]{0:T(128)} %param.13) | copy-start | bytes 1540
  9.2 39.9 %copy-start.6 = (f32[128]{0:T(128)S(1)}, f32[128]{0:T(128)}, u32[]{:S(2)}) copy-start(f32[128]{0:T(128)} %param.12) | copy-start | bytes 1540
  10.5 4.9 %collective-permute-start = (f32[200]{0:T(256)S(1)}, f32[200]{0:T(256)S(1)}, u32[]{:S(2)}, u32[]{:S(2)}) collective-permute-start(f32[200]{0:T(256)S(1)} %multiply_reduce_fusion.1), channel_id=1, source_target_pairs={{0,1},{1,0},{2,3},{3,2},{4,5},{5,4},{6,7},{7,6},{8,9},{9,8},{10,11... | collective-permute-start | bytes 2408 | tf_op jit(solution)/shard_map/ppermute | solution.py:18
  15.3 35.6 %copy-start.4 = (pred[128,400]{0,1:T(8,128)(4,1)S(1)}, pred[128,400]{0,1:T(8,128)(4,1)}, u32[]{:S(2)}) copy-start(pred[128,400]{0,1:T(8,128)(4,1)} %get-tuple-element.20) | copy-start | bytes 153604
  43.4 7.1 %collective-permute-start.1 = (bf16[1600,128]{1,0:T(8,128)(2,1)S(1)}, bf16[1600,128]{1,0:T(8,128)(2,1)S(1)}, u32[]{:S(2)}, u32[]{:S(2)}) collective-permute-start(bf16[1600,128]{1,0:T(8,128)(2,1)S(1)} %all_gather.6), channel_id=1, source_target_pairs={{0,1},{1,0},{2,3},{3,2},{4,5},{5,4},{6,7},{7,6},{8,9},{9,8},{10,11... | collective-permute-start | bytes 1228808 | tf_op jit(solution)/shard_map/ppermute | solution.py:18
  50.2 1.1 copy-start.3
  50.6 1.2 copy-start.1
  50.6 1.6 copy-start.2
Sparse Core Ops, SparseCore 0:
  9.5 129.1 all-gather.1
  145.5 42.1 reduce-scatter.1
where the time goes:
time: 199 us; the launch traced here: 197 us
  waiting for transfers between devices  128 us (64%)
  blocking collectives  27 us (14%)
  between operations  13.7 us (7%)
  matrix products  10.7 us (5%)
  starting transfers between devices  6.52 us (3%)
  other arithmetic  5.8 us (3%)
  local copies, waits for them, and re-layouts  4.86 us (2%)
    all_gather x1, waiting for transfers between devices, local(): lax.all_gather(out_weight, 'seq', axis=1, tiled=True)  84.8 us
    reduce_scatter x1, waiting for transfers between devices, local(): lax.psum_scatter(partial_value, 'head', scatter_dimension=1, tiled=True)  42.3 us
    all_gather x1, blocking collectives, local(): gathered = lax.all_gather(local_pair, 'seq', axis=0, tiled=True)  27 us
    dot_general x1, matrix products, local(): jnp.dot(attended, lax.all_gather(out_weight, 'seq', axis=1, tiled=True),...  6.67 us
    ppermute x2, starting transfers between devices, swapped(): return lax.ppermute(value, axis, pairs)  6.48 us
  transfers between devices with their start and end apart: 4, of which 3 were waited for; matrix products, arithmetic and copies ran while one was open for 6% of the time, Pallas kernels for 0%

commit v1 on v0

v1 whole, which is shorter than its diff:
```python
import functools
import math

import jax
import jax.numpy as jnp
from jax import lax
from jax.experimental import pallas as pl
from jax.experimental.pallas import tpu as pltpu
from jax.sharding import PartitionSpec as P

HD = 128
TILES = 4
EPSILON = 1e-05
MESH = pl.DeviceIdType.MESH
NT = (((1,), (1,)), ((), ()))
NN = (((1,), (0,)), ((), ()))
CHUNK = 1024


def dot(x, y, dims=NN):
    return lax.dot_general(x, y, dims, preferred_element_type=jnp.float32)


def kernel(
    ns, nh, q_ref, x_ref, w_ref, ow_ref, qg_ref, kg_ref, cnt_ref, span_ref, out_ref,
    acc, sq_own, sq_other, kv, att, keep, send0, recv0, sends, recvs, fin, pieces,
    sq_ss, sq_rs, kv_ss, kv_rs, a_ss, a_rs, l_ss, l_rs, f_ss, f_rs,
):
    seq = lax.axis_index("seq")
    head = lax.axis_index("head")
    ratio = ns // nh
    levels = int(math.log2(nh))
    chain = ns // 2
    place, side = seq // 2, seq % 2
    core = head % 2
    rows = q_ref.shape[0]
    heads_here = q_ref.shape[1] // HD
    vis = x_ref.shape[0]
    pad = kv.shape[2]
    half = ow_ref.shape[1] // 2
    mate = head + 1 - 2 * core
    across = seq + 1 - 2 * side
    has_left, has_right = place > 0, place < chain - 1

    def bit(level):
        return (head // 2**level) % 2

    def partner(level):
        return head + 2**level * (1 - 2 * bit(level))

    barrier = pltpu.get_barrier_semaphore()

    def greet(s, h):
        pl.semaphore_signal(barrier, inc=1, device_id=(s, h), device_id_type=MESH)

    @pl.when(has_left)
    def _():
        greet(seq - 2, head)

    @pl.when(has_right)
    def _():
        greet(seq + 2, head)

    greet(across, head)
    for level in range(levels):
        greet(seq, partner(level))
    for j in range(ratio):
        for h in range(nh):
            source = ratio * head + j

            @pl.when(jnp.logical_or(source != seq, head != h))
            def _():
                greet(source, h)

    acc[...] = jnp.zeros_like(acc)

    def project(i, carry):
        at = pl.ds(pl.multiple_of(i * CHUNK, CHUNK), CHUNK)
        acc[0:vis, :] += dot(x_ref[:, at], w_ref[:, at], NT)
        return carry

    lax.fori_loop(0, x_ref.shape[1] // CHUNK, project, 0)
    raw = acc[...]
    lane = lax.broadcasted_iota(jnp.int32, (1, HD), 1)
    low = lane < HD // 2
    squares = jnp.sum(jnp.where(low, raw * raw, 0.0), axis=1, keepdims=True)
    sq_own[...] = jnp.broadcast_to(squares, sq_own.shape)

    expected = (
        jnp.where(has_left, 1, 0) + jnp.where(has_right, 1, 0) + 1 + levels + ns
        - jnp.where(seq // ratio == head, 1, 0)
    )
    pl.semaphore_wait(barrier, expected)

    sq_copy = pltpu.make_async_remote_copy(
        src_ref=sq_own, dst_ref=sq_other, send_sem=sq_ss, recv_sem=sq_rs,
        device_id=(seq, mate), device_id_type=MESH,
    )
    sq_copy.start()
    left_half, right_half = [], []
    for h in range(heads_here):
        field = q_ref[:, h * HD : (h + 1) * HD].astype(jnp.float32)
        mean_sq = jnp.mean(field * field, axis=1, keepdims=True)
        normed = field / jnp.sqrt(mean_sq + EPSILON) * qg_ref[...]
        swapped = pltpu.roll(normed, HD // 2, 1)
        left_half.append(jnp.where(low, 0.0, swapped).astype(jnp.bfloat16))
        right_half.append(jnp.where(low, swapped, 0.0).astype(jnp.bfloat16))
    sq_copy.wait()
    inverse = 1.0 / jnp.sqrt((sq_own[...] + sq_other[...]) / HD + EPSILON)
    gain = kg_ref[...]
    gain = jnp.where(core == 0, gain, pltpu.roll(gain, HD // 2, 1))
    block = jnp.where(low, raw * inverse * gain, raw)
    block = jnp.where(core == 0, pltpu.roll(block, HD // 2, 1), block)
    kv[core, seq] = block.astype(jnp.bfloat16)

    def nearest(i):
        both = jnp.minimum(place, chain - 1 - place)
        t = (i + 1) // 2
        near = jnp.where(i % 2 == 1, place - t, place + t)
        far = jnp.where(has_right & (place < chain - 1 - place), place + (i - both), place - (i - both))
        return jnp.where(i <= 2 * both, near, far)

    def kv_copy(s, kind, target):
        return pltpu.make_async_remote_copy(
            src_ref=kv.at[core, s], dst_ref=kv.at[core, s],
            send_sem=kv_ss.at[s, kind], recv_sem=kv_rs.at[core, s],
            device_id=target, device_id_type=MESH,
        )

    def a_copy(s, kind, target):
        return pltpu.make_async_remote_copy(
            src_ref=att.at[s], dst_ref=att.at[s],
            send_sem=a_ss.at[s, kind], recv_sem=a_rs.at[s],
            device_id=target, device_id_type=MESH,
        )

    def onward(copy, at, s, act):
        @pl.when(jnp.logical_and(at <= place, has_right))
        def _():
            act(copy(s, 0, (seq + 2, head)))

        @pl.when(jnp.logical_and(at >= place, has_left))
        def _():
            act(copy(s, 1, (seq - 2, head)))

        act(copy(s, 2, (across, head)))

    def start(copy):
        copy.start()

    def wait_send(copy):
        copy.wait_send()

    def kv_step(i, carry):
        @pl.when(i < chain)
        def _():
            at = nearest(i)
            s = 2 * at + side

            @pl.when(i > 0)
            def _():
                kv_copy(s, 3, (seq, mate)).wait_recv()

            onward(kv_copy, at, s, start)
            kv_copy(s, 3, (seq, mate)).start()

        @pl.when(i > 0)
        def _():
            s = 2 * nearest(i - 1) + 1 - side
            kv_copy(s, 3, (seq, mate)).wait_recv()
            kv_copy(s, 3, (seq, mate)).start()

        return carry

    lax.fori_loop(0, chain + 1, kv_step, 0)

    def kv_from_mate(s, carry):
        pltpu.make_async_remote_copy(
            src_ref=kv.at[1 - core, s], dst_ref=kv.at[1 - core, s],
            send_sem=kv_ss.at[s, 3], recv_sem=kv_rs.at[1 - core, s],
            device_id=(seq, mate), device_id_type=MESH,
        ).wait_recv()
        return carry

    lax.fori_loop(0, ns, kv_from_mate, 0)

    slots = ns * pad
    cap = ns * vis // TILES
    j = lax.broadcasted_iota(jnp.int32, (1, slots), 1)
    owner = ((j.astype(jnp.float32) + 0.5) * (1.0 / pad)).astype(jnp.int32)
    inside = j - owner * pad
    token = owner * vis + inside
    tile = jnp.zeros_like(token)
    count = jnp.full_like(token, cnt_ref[0])
    for t in range(1, TILES):
        tile = jnp.where(token >= t * cap, t, tile)
        count = jnp.where(token >= t * cap, t * cap + cnt_ref[t], count)
    present = jnp.logical_and(inside < vis, token < count)
    tile = jnp.where(present, tile, 2 * TILES).astype(jnp.float32)
    span_f = span_ref[...].astype(jnp.float32)
    first = jnp.transpose(jnp.broadcast_to(span_f[0:1, :], (HD, rows)))[:, 0:1]
    end = jnp.transpose(jnp.broadcast_to(span_f[1:2, :], (HD, rows)))[:, 0:1]
    allowed = jnp.logical_and(first <= tile, tile < end)
    scale = math.log2(math.e) / math.sqrt(HD)
    both = jnp.concatenate(
        [kv[0].reshape(slots, HD), kv[1].reshape(slots, HD)], axis=1
    )
    for h in range(heads_here):
        query = jnp.concatenate([left_half[h], right_half[h]], axis=1)
        weights = jnp.where(allowed, jnp.exp2(dot(query, both, NT) * scale), 0.0)
        total = jnp.sum(weights, axis=1, keepdims=True)
        numer = dot(weights.astype(jnp.bfloat16), both)
        numer = jnp.where(low, numer[:, :HD], numer[:, HD:])
        att[seq, :, h * HD : (h + 1) * HD] = (numer / total).astype(jnp.bfloat16)

    def level_refs(level):
        if level == 0:
            return send0, recv0
        return sends[level - 1], recvs[level - 1]

    def level_copy(level, s):
        source, target = level_refs(level)
        return pltpu.make_async_remote_copy(
            src_ref=source.at[s], dst_ref=target.at[s],
            send_sem=l_ss.at[level, s], recv_sem=l_rs.at[level, s],
            device_id=(seq, partner(level)), device_id_type=MESH,
        )

    def final_copy(s):
        return pltpu.make_async_remote_copy(
            src_ref=fin.at[s], dst_ref=pieces.at[seq % ratio, head],
            send_sem=f_ss.at[s], recv_sem=f_rs.at[seq % ratio, head],
            device_id=(s, seq // ratio), device_id_type=MESH,
        )

    def is_mine(s):
        return jnp.logical_and(s == seq, seq // ratio == head)

    def turn(i):
        chained = jnp.where(i == 0, 0, (i + 1) // 2)
        swapped = jnp.where(i == ns - 1, chain - 1, jnp.maximum(i // 2 - 1, 0))
        own_side = jnp.logical_or(i == 0, jnp.logical_and(i % 2 == 1, i < ns - 1))
        at = nearest(jnp.where(own_side, chained, swapped))
        return at, 2 * at + jnp.where(own_side, side, 1 - side), own_side

    sizes = [rows] + [rows >> level for level in range(1, levels)]

    def kept_at(level):
        off = 0
        for done in range(1, level + 1):
            off = off + bit(done) * sizes[done]
        return off

    def first_stage(i):
        at, s, own_side = turn(i)

        @pl.when(i > 0)
        def _():
            a_copy(s, 2, (across, head)).wait_recv()

        @pl.when(own_side)
        def _():
            onward(a_copy, at, s, start)

        rows_in = att[s]
        other = pl.ds(pl.multiple_of((1 - core) * half, half), half)
        send0[s] = dot(rows_in, ow_ref[:, other]).astype(jnp.bfloat16)
        level_copy(0, s).start()
        mine = pl.ds(pl.multiple_of(core * half, half), half)
        keep[s] = dot(rows_in, ow_ref[:, mine])

    def later_stage(level, i):
        _, s, _ = turn(i)
        level_copy(level - 1, s).wait_recv()
        size = sizes[level - 1]
        base = kept_at(level - 1)
        arrived = level_refs(level - 1)[1]
        if level == levels:
            total = keep[s, pl.ds(pl.multiple_of(base, size), size)] + arrived[s].astype(jnp.float32)
            fin[s] = total.astype(jnp.bfloat16)

            @pl.when(is_mine(s))
            def _():
                pieces[seq % ratio, head] = fin[s]

            @pl.when(jnp.logical_not(is_mine(s)))
            def _():
                final_copy(s).start()

        else:
            step = sizes[level]
            out_off = (1 - bit(level)) * step
            in_off = bit(level) * step
            sent = keep[s, pl.ds(pl.multiple_of(base + out_off, step), step)]
            sent = sent + arrived[s, pl.ds(pl.multiple_of(out_off, step), step)].astype(jnp.float32)
            level_refs(level)[0][s] = sent.astype(jnp.bfloat16)
            level_copy(level, s).start()
            at = pl.ds(pl.multiple_of(base + in_off, step), step)
            keep[s, at] = keep[s, at] + arrived[s, pl.ds(pl.multiple_of(in_off, step), step)].astype(jnp.float32)

    def pipeline(i, carry):
        for level in range(levels, 0, -1):
            @pl.when(jnp.logical_and(i >= level, i - level < ns))
            def _():
                later_stage(level, i - level)

        @pl.when(i < ns)
        def _():
            first_stage(i)

        return carry

    lax.fori_loop(0, ns + levels, pipeline, 0)

    for b in range(ratio):
        for h in range(nh):
            @pl.when(jnp.logical_or(ratio * head + b != seq, head != h))
            def _():
                pltpu.make_async_remote_copy(
                    src_ref=fin.at[0], dst_ref=pieces.at[b, h],
                    send_sem=f_ss.at[0], recv_sem=f_rs.at[b, h],
                    device_id=(across, head), device_id_type=MESH,
                ).wait_recv()

            off = sum(((h >> level) & 1) * sizes[level] for level in range(1, levels))
            col = b * 2 * half + (h & 1) * half
            out_ref[off : off + sizes[-1], col : col + half] = pieces[b, h]

    def finish(s, carry):
        at = s // 2

        @pl.when(s % 2 == side)
        def _():
            onward(kv_copy, at, s, wait_send)
            onward(a_copy, at, s, wait_send)

        kv_copy(s, 3, (seq, mate)).wait_send()
        for level in range(levels):
            level_copy(level, s).wait_send()

        @pl.when(jnp.logical_not(is_mine(s)))
        def _():
            final_copy(s).wait_send()

        return carry

    lax.fori_loop(0, ns, finish, 0)


def local(queries, vision, kv_weight, out_weight, q_gain, k_gain, tile_counts, spans):
    ns, nh = lax.axis_size("seq"), lax.axis_size("head")
    rows, width = queries.shape
    vis, model = vision.shape
    cols = out_weight.shape[1]
    half = cols // 2
    levels = int(math.log2(nh))
    pad = -(-vis // 16) * 16
    weights = jnp.swapaxes(kv_weight, 1, 2).reshape(-1, model)
    bf16, f32 = jnp.bfloat16, jnp.float32
    halved = [pltpu.VMEM((ns, rows >> level, half), bf16) for level in range(1, levels)]
    last = rows >> (levels - 1)
    vmem = pl.BlockSpec(memory_space=pltpu.VMEM)
    dma = pltpu.SemaphoreType.DMA
    return pl.pallas_call(
        functools.partial(kernel, ns, nh),
        out_shape=jax.ShapeDtypeStruct((rows, model // nh), bf16),
        in_specs=[vmem] * 6 + [pl.BlockSpec(memory_space=pltpu.SMEM), vmem],
        out_specs=vmem,
        scratch_shapes=[
            pltpu.VMEM((pad, HD), f32),
            pltpu.VMEM((pad, HD), f32),
            pltpu.VMEM((pad, HD), f32),
            pltpu.VMEM((2, ns, pad, HD), bf16),
            pltpu.VMEM((ns, rows, width), bf16),
            pltpu.VMEM((ns, rows, half), f32),
            pltpu.VMEM((ns, rows, half), bf16),
            pltpu.VMEM((ns, rows, half), bf16),
            halved,
            list(halved),
            pltpu.VMEM((ns, last, half), bf16),
            pltpu.VMEM((ns // nh, nh, last, half), bf16),
            dma, dma, dma((ns, 4)), dma((2, ns)), dma((ns, 3)), dma((ns,)),
            dma((levels, ns)), dma((levels, ns)), dma((ns,)), dma((ns // nh, nh)),
        ],
        compiler_params=pltpu.CompilerParams(
            collective_id=0, has_side_effects=True, vmem_limit_bytes=48 * 2**20
        ),
    )(
        queries, vision, weights, out_weight, q_gain.reshape(1, HD), k_gain.reshape(1, HD),
        tile_counts, jnp.swapaxes(spans, 0, 1),
    )


def solution(mesh):
    return jax.shard_map(
        local,
        mesh=mesh,
        in_specs=(
            P("seq", "head"),
            P("seq", None),
            P(None, None, "head"),
            P("head", "seq"),
            P(),
            P(),
            P(),
            P("seq", None),
        ),
        out_specs=P("seq", "head"),
        check_vma=False,
    )
```

time: 199 us -> 72.2 us (0.36)
  the two profiles are of different devices: /device:TPU:3 before, /device:TPU:28 now
where the time goes in v1:
time: 72.2 us; the launch traced here: 71.9 us
  Pallas kernels  64.7 us (90%)
  local copies, waits for them, and re-layouts  7.16 us (10%)
    pallas_call x1, Pallas kernels, local(): pl.pallas_call(functools.partial(kernel, ns, nh), out_shape=jax.ShapeDtyp...  64.7 us
    unnamed x15, local copies, waits for them, and re-layouts  7.16 us

profile of v1, /device:TPU:28, one launch (start us, length us, event | category | flops | bytes accessed | tf_op | source)
XLA Modules:
  0.0 71.9 jit_solution(17422845581608173219)
XLA Ops:
  0.0 0.0 copy-start
  0.0 1.6 %copy-done = bf16[2,8192,64]{1,2,0:T(8,128)(2,1)S(1)} copy-done((bf16[2,8192,64]{1,2,0:T(8,128)(2,1)S(1)}, bf16[2,8192,64]{1,2,0:T(8,128)(2,1)}, u32[]{:S(2)}) %copy-start) | copy-done | bytes 2097176
  1.6 0.0 copy-start.1
  1.6 1.2 %copy-done.1 = bf16[512,1024]{1,0:T(8,128)(2,1)S(1)} copy-done((bf16[512,1024]{1,0:T(8,128)(2,1)S(1)}, bf16[512,1024]{1,0:T(8,128)(2,1)}, u32[]{:S(2)}) %copy-start.1) | copy-done | bytes 1048600
  2.8 0.0 copy-start.2
  2.8 0.9 %copy-done.2 = bf16[128,512]{1,0:T(8,128)(2,1)S(1)} copy-done((bf16[128,512]{1,0:T(8,128)(2,1)S(1)}, bf16[128,512]{1,0:T(8,128)(2,1)}, u32[]{:S(2)}) %copy-start.2) | copy-done | bytes 131096
  3.7 0.0 copy-start.3
  3.7 0.7 copy-done.3
  4.4 0.0 copy-start.4
  4.4 0.7 copy-done.4
  5.1 0.0 copy-start.5
  5.1 0.7 copy-done.5
  5.7 0.0 copy-start.6
  5.7 0.7 copy-done.6
  6.4 64.7 %shard_map.82 = bf16[128,2048]{1,0:T(8,128)(2,1)S(1)} custom-call(bf16[128,512]{1,0:T(8,128)(2,1)S(1)} %copy-done.2, bf16[200,8192]{1,0:T(8,128)(2,1)} %x_ref.1, bf16[128,8192]{1,0:T(8,128)(2,1)S(1)} %bitcast.6, bf16[512,1024]{1,0:T(8,128)(2,1)S(1)} %copy-done.1, f32[1,128]{1,0:T(1,128)S(1)} %bitcast.8, f32[1,128]{1,0:T(1,128)S(1)} %bitcast.9, ...), custom_call_target="tpu_custom_call" | custom-call | tf_op jit(solution)/shard_map/pallas_call | solution.py:364
  71.1 0.8 %copy.10 = bf16[128,2048]{1,0:T(8,128)(2,1)} copy(bf16[128,2048]{1,0:T(8,128)(2,1)S(1)} %shard_map.82) | data formatting | bytes 1048576
Async XLA Ops:
  0.0 1.6 %copy-start = (bf16[2,8192,64]{1,2,0:T(8,128)(2,1)S(1)}, bf16[2,8192,64]{1,2,0:T(8,128)(2,1)}, u32[]{:S(2)}) copy-start(bf16[2,8192,64]{1,2,0:T(8,128)(2,1)} %param.10) | copy-start | bytes 6291460
  1.6 1.2 %copy-start.1 = (bf16[512,1024]{1,0:T(8,128)(2,1)S(1)}, bf16[512,1024]{1,0:T(8,128)(2,1)}, u32[]{:S(2)}) copy-start(bf16[512,1024]{1,0:T(8,128)(2,1)} %ow_ref.1) | copy-start | bytes 3145732
  2.8 0.9 %copy-start.2 = (bf16[128,512]{1,0:T(8,128)(2,1)S(1)}, bf16[128,512]{1,0:T(8,128)(2,1)}, u32[]{:S(2)}) copy-start(bf16[128,512]{1,0:T(8,128)(2,1)} %q_ref.1) | copy-start | bytes 393220
  3.7 0.7 copy-start.3
  4.4 0.7 copy-start.4
  5.1 0.7 copy-start.5
  5.7 0.7 copy-start.6

commit v2 on v1

--- a/solution.py
+++ b/solution.py
@@ -22,8 +22,9 @@
 
 
 def kernel(
-    ns, nh, q_ref, x_ref, w_ref, ow_ref, qg_ref, kg_ref, cnt_ref, span_ref, out_ref,
-    acc, sq_own, sq_other, kv, att, keep, send0, recv0, sends, recvs, fin, pieces,
+    ns, nh, q_hbm, x_hbm, w_hbm, ow_hbm, qg_hbm, kg_hbm, cnt_hbm, span_hbm, out_ref,
+    q_ref, x_ref, w_ref, ow_ref, qg_ref, kg_ref, cnt_ref, span_ref, in_sem, x_sem, w_sem,
+    numer, wsum, acc, sq_own, sq_other, kv, att, keep, send0, recv0, sends, recvs, fin, pieces,
     sq_ss, sq_rs, kv_ss, kv_rs, a_ss, a_rs, l_ss, l_rs, f_ss, f_rs,
 ):
     seq = lax.axis_index("seq")
@@ -40,7 +41,6 @@
     half = ow_ref.shape[1] // 2
     mate = head + 1 - 2 * core
     across = seq + 1 - 2 * side
-    has_left, has_right = place > 0, place < chain - 1
 
     def bit(level):
         return (head // 2**level) % 2
@@ -48,19 +48,39 @@
     def partner(level):
         return head + 2**level * (1 - 2 * bit(level))
 
+    chunks = x_ref.shape[1] // CHUNK
+
+    def x_copy(i):
+        at = pl.ds(pl.multiple_of(i * CHUNK, CHUNK), CHUNK)
+        return pltpu.make_async_copy(x_hbm.at[:, at], x_ref.at[:, at], x_sem.at[i])
+
+    def w_copy(i):
+        at = pl.ds(pl.multiple_of(i * CHUNK, CHUNK), CHUNK)
+        return pltpu.make_async_copy(w_hbm.at[:, at], w_ref.at[:, at], w_sem.at[i])
+
+    small = [
+        pltpu.make_async_copy(source, target, in_sem.at[i])
+        for i, (source, target) in enumerate([
+            (q_hbm, q_ref), (qg_hbm, qg_ref), (kg_hbm, kg_ref), (cnt_hbm, cnt_ref),
+            (span_hbm, span_ref), (ow_hbm, ow_ref),
+        ])
+    ]
+    for i in range(chunks):
+        x_copy(i).start()
+        w_copy(i).start()
+    for copy in small:
+        copy.start()
+
     barrier = pltpu.get_barrier_semaphore()
 
     def greet(s, h):
         pl.semaphore_signal(barrier, inc=1, device_id=(s, h), device_id_type=MESH)
 
-    @pl.when(has_left)
-    def _():
-        greet(seq - 2, head)
-
-    @pl.when(has_right)
-    def _():
-        greet(seq + 2, head)
-
+    def greet_chain(k, carry):
+        greet(2 * lax.rem(place + k, chain) + side, head)
+        return carry
+
+    lax.fori_loop(1, chain, greet_chain, 0)
     greet(across, head)
     for level in range(levels):
         greet(seq, partner(level))
@@ -75,11 +95,13 @@
     acc[...] = jnp.zeros_like(acc)
 
     def project(i, carry):
+        x_copy(i).wait()
+        w_copy(i).wait()
         at = pl.ds(pl.multiple_of(i * CHUNK, CHUNK), CHUNK)
         acc[0:vis, :] += dot(x_ref[:, at], w_ref[:, at], NT)
         return carry
 
-    lax.fori_loop(0, x_ref.shape[1] // CHUNK, project, 0)
+    lax.fori_loop(0, chunks, project, 0)
     raw = acc[...]
     lane = lax.broadcasted_iota(jnp.int32, (1, HD), 1)
     low = lane < HD // 2
@@ -87,7 +109,7 @@
     sq_own[...] = jnp.broadcast_to(squares, sq_own.shape)
 
     expected = (
-        jnp.where(has_left, 1, 0) + jnp.where(has_right, 1, 0) + 1 + levels + ns
+        chain + levels + ns
         - jnp.where(seq // ratio == head, 1, 0)
     )
     pl.semaphore_wait(barrier, expected)
@@ -97,6 +119,8 @@
         device_id=(seq, mate), device_id_type=MESH,
     )
     sq_copy.start()
+    for copy in small[:-1]:
+        copy.wait()
     left_half, right_half = [], []
     for h in range(heads_here):
         field = q_ref[:, h * HD : (h + 1) * HD].astype(jnp.float32)
@@ -117,7 +141,7 @@
         both = jnp.minimum(place, chain - 1 - place)
         t = (i + 1) // 2
         near = jnp.where(i % 2 == 1, place - t, place + t)
-        far = jnp.where(has_right & (place < chain - 1 - place), place + (i - both), place - (i - both))
+        far = jnp.where(place < chain - 1 - place, place + (i - both), place - (i - both))
         return jnp.where(i <= 2 * both, near, far)
 
     def kv_copy(s, kind, target):
@@ -134,16 +158,15 @@
             device_id=target, device_id_type=MESH,
         )
 
-    def onward(copy, at, s, act):
-        @pl.when(jnp.logical_and(at <= place, has_right))
-        def _():
-            act(copy(s, 0, (seq + 2, head)))
-
-        @pl.when(jnp.logical_and(at >= place, has_left))
-        def _():
-            act(copy(s, 1, (seq - 2, head)))
-
-        act(copy(s, 2, (across, head)))
+    def spread(copy, act):
+        act(copy(seq, chain, (across, head)))
+
+        def one(i, carry):
+            at = nearest(i)
+            act(copy(seq, at, (2 * at + side, head)))
+            return carry
+
+        lax.fori_loop(1, chain, one, 0)
 
     def start(copy):
         copy.start()
@@ -151,67 +174,72 @@
     def wait_send(copy):
         copy.wait_send()
 
-    def kv_step(i, carry):
-        @pl.when(i < chain)
-        def _():
-            at = nearest(i)
-            s = 2 * at + side
-
-            @pl.when(i > 0)
-            def _():
-                kv_copy(s, 3, (seq, mate)).wait_recv()
-
-            onward(kv_copy, at, s, start)
-            kv_copy(s, 3, (seq, mate)).start()
-
-        @pl.when(i > 0)
-        def _():
-            s = 2 * nearest(i - 1) + 1 - side
-            kv_copy(s, 3, (seq, mate)).wait_recv()
-            kv_copy(s, 3, (seq, mate)).start()
-
-        return carry
-
-    lax.fori_loop(0, chain + 1, kv_step, 0)
-
-    def kv_from_mate(s, carry):
-        pltpu.make_async_remote_copy(
-            src_ref=kv.at[1 - core, s], dst_ref=kv.at[1 - core, s],
-            send_sem=kv_ss.at[s, 3], recv_sem=kv_rs.at[1 - core, s],
-            device_id=(seq, mate), device_id_type=MESH,
-        ).wait_recv()
-        return carry
-
-    lax.fori_loop(0, ns, kv_from_mate, 0)
-
-    slots = ns * pad
+    slots = jnp.concatenate(
+        [jnp.concatenate([left, right], axis=1) for left, right in zip(left_half, right_half)], axis=0
+    )
     cap = ns * vis // TILES
-    j = lax.broadcasted_iota(jnp.int32, (1, slots), 1)
-    owner = ((j.astype(jnp.float32) + 0.5) * (1.0 / pad)).astype(jnp.int32)
-    inside = j - owner * pad
-    token = owner * vis + inside
-    tile = jnp.zeros_like(token)
-    count = jnp.full_like(token, cnt_ref[0])
-    for t in range(1, TILES):
-        tile = jnp.where(token >= t * cap, t, tile)
-        count = jnp.where(token >= t * cap, t * cap + cnt_ref[t], count)
-    present = jnp.logical_and(inside < vis, token < count)
-    tile = jnp.where(present, tile, 2 * TILES).astype(jnp.float32)
     span_f = span_ref[...].astype(jnp.float32)
     first = jnp.transpose(jnp.broadcast_to(span_f[0:1, :], (HD, rows)))[:, 0:1]
     end = jnp.transpose(jnp.broadcast_to(span_f[1:2, :], (HD, rows)))[:, 0:1]
-    allowed = jnp.logical_and(first <= tile, tile < end)
+    first = jnp.concatenate([first] * heads_here, axis=0)
+    end = jnp.concatenate([end] * heads_here, axis=0)
     scale = math.log2(math.e) / math.sqrt(HD)
-    both = jnp.concatenate(
-        [kv[0].reshape(slots, HD), kv[1].reshape(slots, HD)], axis=1
-    )
+    numer[...] = jnp.zeros_like(numer)
+    wsum[...] = jnp.zeros_like(wsum)
+
+    def attend(s):
+        pltpu.make_async_remote_copy(
+            src_ref=kv.at[1 - core, s], dst_ref=kv.at[1 - core, s],
+            send_sem=kv_ss.at[s, chain + 1], recv_sem=kv_rs.at[1 - core, s],
+            device_id=(seq, mate), device_id_type=MESH,
+        ).wait_recv()
+        inside = lax.broadcasted_iota(jnp.int32, (1, pad), 1)
+        token = inside + s * vis
+        tile = jnp.zeros_like(token)
+        count = jnp.full_like(token, cnt_ref[0])
+        for t in range(1, TILES):
+            tile = jnp.where(token >= t * cap, t, tile)
+            count = jnp.where(token >= t * cap, t * cap + cnt_ref[t], count)
+        present = jnp.logical_and(inside < vis, token < count)
+        tile = jnp.where(present, tile, 2 * TILES).astype(jnp.float32)
+        allowed = jnp.logical_and(first <= tile, tile < end)
+        both = jnp.concatenate([kv[0, s], kv[1, s]], axis=1)
+        weights = jnp.where(allowed, jnp.exp2(dot(slots, both, NT) * scale), 0.0)
+        wsum[...] += weights
+        numer[...] += dot(weights.astype(jnp.bfloat16), both)
+
+    spread(kv_copy, start)
+    kv_copy(seq, chain + 1, (seq, mate)).start()
+
+    def kv_step(i, carry):
+        @pl.when(jnp.logical_and(i > 0, i < chain))
+        def _():
+            s = 2 * nearest(i) + side
+            kv_copy(s, chain, (across, head)).wait_recv()
+            kv_copy(s, chain, (across, head)).start()
+            kv_copy(s, chain + 1, (seq, mate)).start()
+
+        @pl.when(jnp.logical_and(i > 0, i <= chain))
+        def _():
+            attend(2 * nearest(i - 1) + side)
+            s = 2 * nearest(i - 1) + 1 - side
+            kv_copy(s, chain + 1, (seq, mate)).wait_recv()
+            kv_copy(s, chain + 1, (seq, mate)).start()
+
+        @pl.when(i > 1)
+        def _():
+            attend(2 * nearest(i - 2) + 1 - side)
+
+        return carry
+
+    lax.fori_loop(1, chain + 2, kv_step, 0)
     for h in range(heads_here):
-        query = jnp.concatenate([left_half[h], right_half[h]], axis=1)
-        weights = jnp.where(allowed, jnp.exp2(dot(query, both, NT) * scale), 0.0)
-        total = jnp.sum(weights, axis=1, keepdims=True)
-        numer = dot(weights.astype(jnp.bfloat16), both)
-        numer = jnp.where(low, numer[:, :HD], numer[:, HD:])
-        att[seq, :, h * HD : (h + 1) * HD] = (numer / total).astype(jnp.bfloat16)
+        at = slice(h * rows, (h + 1) * rows)
+        total = jnp.sum(wsum[at], axis=1, keepdims=True)
+        mixed = jnp.where(low, numer[at, :HD], numer[at, HD:])
+        att[seq, :, h * HD : (h + 1) * HD] = (mixed / total).astype(jnp.bfloat16)
+    small[-1].wait()
+    spread(a_copy, start)
 
     def level_refs(level):
         if level == 0:
@@ -241,7 +269,7 @@
         swapped = jnp.where(i == ns - 1, chain - 1, jnp.maximum(i // 2 - 1, 0))
         own_side = jnp.logical_or(i == 0, jnp.logical_and(i % 2 == 1, i < ns - 1))
         at = nearest(jnp.where(own_side, chained, swapped))
-        return at, 2 * at + jnp.where(own_side, side, 1 - side), own_side
+        return 2 * at + jnp.where(own_side, side, 1 - side), own_side
 
     sizes = [rows] + [rows >> level for level in range(1, levels)]
 
@@ -252,15 +280,15 @@
         return off
 
     def first_stage(i):
-        at, s, own_side = turn(i)
+        s, own_side = turn(i)
 
         @pl.when(i > 0)
         def _():
-            a_copy(s, 2, (across, head)).wait_recv()
-
-        @pl.when(own_side)
-        def _():
-            onward(a_copy, at, s, start)
+            a_copy(s, chain, (across, head)).wait_recv()
+
+        @pl.when(jnp.logical_and(own_side, i > 0))
+        def _():
+            a_copy(s, chain, (across, head)).start()
 
         rows_in = att[s]
         other = pl.ds(pl.multiple_of((1 - core) * half, half), half)
@@ -270,7 +298,7 @@
         keep[s] = dot(rows_in, ow_ref[:, mine])
 
     def later_stage(level, i):
-        _, s, _ = turn(i)
+        s, _ = turn(i)
         level_copy(level - 1, s).wait_recv()
         size = sizes[level - 1]
         base = kept_at(level - 1)
@@ -299,18 +327,28 @@
             keep[s, at] = keep[s, at] + arrived[s, pl.ds(pl.multiple_of(in_off, step), step)].astype(jnp.float32)
 
     def pipeline(i, carry):
-        for level in range(levels, 0, -1):
-            @pl.when(jnp.logical_and(i >= level, i - level < ns))
+        @pl.when(i == 1)
+        def _():
+            later_stage(1, 0)
+
+        @pl.when(i < ns)
+        def _():
+            first_stage(i)
+
+        @pl.when(jnp.logical_and(i >= 2, i - 1 < ns))
+        def _():
+            later_stage(1, i - 1)
+
+        for level in range(2, levels + 1):
+            lag = 2 * level - 1
+
+            @pl.when(jnp.logical_and(i >= lag, i - lag < ns))
             def _():
-                later_stage(level, i - level)
-
-        @pl.when(i < ns)
-        def _():
-            first_stage(i)
+                later_stage(level, i - lag)
 
         return carry
 
-    lax.fori_loop(0, ns + levels, pipeline, 0)
+    lax.fori_loop(0, ns + 2 * levels - 1, pipeline, 0)
 
     for b in range(ratio):
         for h in range(nh):
@@ -327,14 +365,12 @@
             out_ref[off : off + sizes[-1], col : col + half] = pieces[b, h]
 
     def finish(s, carry):
-        at = s // 2
-
-        @pl.when(s % 2 == side)
-        def _():
-            onward(kv_copy, at, s, wait_send)
-            onward(a_copy, at, s, wait_send)
-
-        kv_copy(s, 3, (seq, mate)).wait_send()
+        @pl.when(jnp.logical_and(s % 2 == side, s != seq))
+        def _():
+            kv_copy(s, chain, (across, head)).wait_send()
+            a_copy(s, chain, (across, head)).wait_send()
+
+        kv_copy(s, chain + 1, (seq, mate)).wait_send()
         for level in range(levels):
             level_copy(level, s).wait_send()
 
@@ -345,6 +381,8 @@
         return carry
 
     lax.fori_loop(0, ns, finish, 0)
+    spread(kv_copy, wait_send)
+    spread(a_copy, wait_send)
 
 
 def local(queries, vision, kv_weight, out_weight, q_gain, k_gain, tile_counts, spans):
@@ -364,9 +402,20 @@
     return pl.pallas_call(
         functools.partial(kernel, ns, nh),
         out_shape=jax.ShapeDtypeStruct((rows, model // nh), bf16),
-        in_specs=[vmem] * 6 + [pl.BlockSpec(memory_space=pltpu.SMEM), vmem],
+        in_specs=[pl.BlockSpec(memory_space=pltpu.HBM)] * 8,
         out_specs=vmem,
         scratch_shapes=[
+            pltpu.VMEM((rows, width), bf16),
+            pltpu.VMEM((vis, model), bf16),
+            pltpu.VMEM((HD, model), bf16),
+            pltpu.VMEM((width, cols), bf16),
+            pltpu.VMEM((1, HD), f32),
+            pltpu.VMEM((1, HD), f32),
+            pltpu.SMEM((TILES,), jnp.int32),
+            pltpu.VMEM((2, rows), jnp.int32),
+            dma((6,)), dma((model // CHUNK,)), dma((model // CHUNK,)),
+            pltpu.VMEM((rows * width // HD, 2 * HD), f32),
+            pltpu.VMEM((rows * width // HD, pad), f32),
             pltpu.VMEM((pad, HD), f32),
             pltpu.VMEM((pad, HD), f32),
             pltpu.VMEM((pad, HD), f32),
@@ -379,11 +428,11 @@
             list(halved),
             pltpu.VMEM((ns, last, half), bf16),
             pltpu.VMEM((ns // nh, nh, last, half), bf16),
-            dma, dma, dma((ns, 4)), dma((2, ns)), dma((ns, 3)), dma((ns,)),
+            dma, dma, dma((ns, ns // 2 + 2)), dma((2, ns)), dma((ns, ns // 2 + 1)), dma((ns,)),
             dma((levels, ns)), dma((levels, ns)), dma((ns,)), dma((ns // nh, nh)),
         ],
         compiler_params=pltpu.CompilerParams(
-            collective_id=0, has_side_effects=True, vmem_limit_bytes=48 * 2**20
+            collective_id=0, has_side_effects=True, vmem_limit_bytes=60 * 2**20
         ),
     )(
         queries, vision, weights, out_weight, q_gain.reshape(1, HD), k_gain.reshape(1, HD),

time: 72.2 us -> 59.6 us (0.83)
  the two profiles are of different devices: /device:TPU:28 before, /device:TPU:25 now
where the time goes in v2:
time: 59.6 us; the launch traced here: 59.4 us
  Pallas kernels  57.5 us (96%)
  local copies, waits for them, and re-layouts  1.88 us (3%)
    pallas_call x1, Pallas kernels, local(): pl.pallas_call(functools.partial(kernel, ns, nh), out_shape=jax.ShapeDtyp...  57.5 us
    unnamed x1, local copies, waits for them, and re-layouts  1.88 us

profile of v2, /device:TPU:25, one launch (start us, length us, event | category | flops | bytes accessed | tf_op | source)
XLA Modules:
  0.0 59.4 jit_solution(12392915136058397218)
XLA Ops:
  0.0 57.5 %shard_map.82 = bf16[128,2048]{1,0:T(8,128)(2,1)} custom-call(bf16[128,512]{1,0:T(8,128)(2,1)} %q_hbm.1, bf16[200,8192]{1,0:T(8,128)(2,1)} %x_hbm.1, bf16[128,8192]{1,0:T(8,128)(2,1)} %bitcast.6, bf16[512,1024]{1,0:T(8,128)(2,1)} %ow_hbm.1, f32[1,128]{1,0:T(1,128)} %bitcast.8, f32[1,128]{1,0:T(1,128)} %bitcast.9, s32[4]{0:T(128)} %cnt_hbm.1, s32[2,128]{1,0:T(2,128)} %bitcast.7), custom_call_target="tpu_custom_call" | custom-call | tf_op jit(solution)/shard_map/pallas_call | solution.py:402
  57.5 1.9 %copy.10 = bf16[128,2048]{1,0:T(8,128)(2,1)} copy(bf16[128,2048]{1,0:T(8,128)(2,1)} %shard_map.82) | data formatting | bytes 1048576

commit v3 on v2

--- a/solution.py
+++ b/solution.py
@@ -24,8 +24,8 @@
 def kernel(
     ns, nh, q_hbm, x_hbm, w_hbm, ow_hbm, qg_hbm, kg_hbm, cnt_hbm, span_hbm, out_ref,
     q_ref, x_ref, w_ref, ow_ref, qg_ref, kg_ref, cnt_ref, span_ref, in_sem, x_sem, w_sem,
-    numer, wsum, acc, sq_own, sq_other, kv, att, keep, send0, recv0, sends, recvs, fin, pieces,
-    sq_ss, sq_rs, kv_ss, kv_rs, a_ss, a_rs, l_ss, l_rs, f_ss, f_rs,
+    numer, wsum, acc, sq_own, sq_other, kv, att, keep, send0, recv0, sends, recvs, fin, middle, pieces,
+    sq_ss, sq_rs, kv_ss, kv_rs, a_ss, a_rs, l_ss, l_rs, f_ss, f_rs, p_ss, p_rs,
 ):
     seq = lax.axis_index("seq")
     head = lax.axis_index("head")
@@ -84,13 +84,23 @@
     greet(across, head)
     for level in range(levels):
         greet(seq, partner(level))
-    for j in range(ratio):
-        for h in range(nh):
-            source = ratio * head + j
-
-            @pl.when(jnp.logical_or(source != seq, head != h))
-            def _():
-                greet(source, h)
+    def greet_sources(k, carry):
+        owner, rest = k // ratio, k % ratio
+        source = ratio * (2 * owner + core) + rest
+        for h in range(2):
+            @pl.when(jnp.logical_or(source != seq, core != h))
+            def _():
+                greet(source, head - core + h)
+
+        return carry
+
+    lax.fori_loop(0, ns // 2, greet_sources, 0)
+
+    def greet_same_core(k, carry):
+        greet(seq, lax.rem(head + 2 * k, nh))
+        return carry
+
+    lax.fori_loop(1, nh // 2, greet_same_core, 0)
 
     acc[...] = jnp.zeros_like(acc)
 
@@ -109,8 +119,8 @@
     sq_own[...] = jnp.broadcast_to(squares, sq_own.shape)
 
     expected = (
-        chain + levels + ns
-        - jnp.where(seq // ratio == head, 1, 0)
+        chain + levels + ns + nh // 2 - 1
+        - jnp.where((seq // ratio) % 2 == core, 1, 0)
     )
     pl.semaphore_wait(barrier, expected)
 
@@ -137,12 +147,17 @@
     block = jnp.where(core == 0, pltpu.roll(block, HD // 2, 1), block)
     kv[core, seq] = block.astype(jnp.bfloat16)
 
+    mid = chain // 2
+    low_half = place < mid
+    gate = jnp.where(low_half, mid - 1, mid)
+    other_gate = jnp.where(low_half, mid, mid - 1)
+    base_here = jnp.where(low_half, 0, mid)
+
     def nearest(i):
-        both = jnp.minimum(place, chain - 1 - place)
-        t = (i + 1) // 2
-        near = jnp.where(i % 2 == 1, place - t, place + t)
-        far = jnp.where(place < chain - 1 - place, place + (i - both), place - (i - both))
-        return jnp.where(i <= 2 * both, near, far)
+        crossed = jnp.where(low_half, mid + i - 1, mid - i)
+        rest = base_here + (i - mid - 1)
+        rest = jnp.where(rest >= place, rest + 1, rest)
+        return jnp.where(i == 0, place, jnp.where(i <= mid, crossed, rest))
 
     def kv_copy(s, kind, target):
         return pltpu.make_async_remote_copy(
@@ -173,6 +188,22 @@
 
     def wait_send(copy):
         copy.wait_send()
+
+    def to_own_half(s, act):
+        def one(k, carry):
+            at = base_here + lax.rem(place - base_here + k, mid)
+            act(a_copy(s, at, (2 * at + side, head)))
+            return carry
+
+        lax.fori_loop(1, mid, one, 0)
+
+    def spread_attended(act):
+        act(a_copy(seq, other_gate, (2 * other_gate + side, head)))
+        act(a_copy(seq, chain, (across, head)))
+        to_own_half(seq, act)
+
+    def forwards(s):
+        return jnp.logical_and(place == gate, (s // 2 < mid) != low_half)
 
     slots = jnp.concatenate(
         [jnp.concatenate([left, right], axis=1) for left, right in zip(left_half, right_half)], axis=0
@@ -239,7 +270,7 @@
         mixed = jnp.where(low, numer[at, :HD], numer[at, HD:])
         att[seq, :, h * HD : (h + 1) * HD] = (mixed / total).astype(jnp.bfloat16)
     small[-1].wait()
-    spread(a_copy, start)
+    spread_attended(start)
 
     def level_refs(level):
         if level == 0:
@@ -254,15 +285,49 @@
             device_id=(seq, partner(level)), device_id_type=MESH,
         )
 
+    lands = head - core + (seq // ratio) % 2
+
     def final_copy(s):
         return pltpu.make_async_remote_copy(
-            src_ref=fin.at[s], dst_ref=pieces.at[seq % ratio, head],
-            send_sem=f_ss.at[s], recv_sem=f_rs.at[seq % ratio, head],
-            device_id=(s, seq // ratio), device_id_type=MESH,
+            src_ref=fin.at[s], dst_ref=middle.at[seq, core],
+            send_sem=f_ss.at[s], recv_sem=f_rs.at[seq, core],
+            device_id=(s, lands), device_id_type=MESH,
         )
 
     def is_mine(s):
-        return jnp.logical_and(s == seq, seq // ratio == head)
+        return jnp.logical_and(s == seq, (seq // ratio) % 2 == core)
+
+    def middle_wait(s, c):
+        pltpu.make_async_remote_copy(
+            src_ref=fin.at[s], dst_ref=middle.at[s, c],
+            send_sem=f_ss.at[s], recv_sem=f_rs.at[s, c],
+            device_id=(across, head), device_id_type=MESH,
+        ).wait_recv()
+
+    def last_copy(s, c):
+        return pltpu.make_async_remote_copy(
+            src_ref=middle.at[s, c], dst_ref=pieces.at[s % ratio, head - core + c],
+            send_sem=p_ss.at[s, c], recv_sem=p_rs.at[s % ratio, head - core + c],
+            device_id=(seq, s // ratio), device_id_type=MESH,
+        )
+
+    def passes(s):
+        return jnp.logical_and((s // ratio) % 2 == core, s // ratio != head)
+
+    def pass_on(i):
+        s, _ = turn(i)
+
+        @pl.when((s // ratio) % 2 == core)
+        def _():
+            for c in range(2):
+                @pl.when(jnp.logical_or(s != seq, core != c))
+                def _():
+                    middle_wait(s, c)
+
+        @pl.when(passes(s))
+        def _():
+            for c in range(2):
+                last_copy(s, c).start()
 
     def turn(i):
         chained = jnp.where(i == 0, 0, (i + 1) // 2)
@@ -288,6 +353,10 @@
 
         @pl.when(jnp.logical_and(own_side, i > 0))
         def _():
+            @pl.when(forwards(s))
+            def _():
+                to_own_half(s, start)
+
             a_copy(s, chain, (across, head)).start()
 
         rows_in = att[s]
@@ -309,7 +378,7 @@
 
             @pl.when(is_mine(s))
             def _():
-                pieces[seq % ratio, head] = fin[s]
+                middle[seq, core] = fin[s]
 
             @pl.when(jnp.logical_not(is_mine(s)))
             def _():
@@ -346,29 +415,41 @@
             def _():
                 later_stage(level, i - lag)
 
-        return carry
-
-    lax.fori_loop(0, ns + 2 * levels - 1, pipeline, 0)
+        @pl.when(i >= 2 * levels + 1)
+        def _():
+            pass_on(i - 2 * levels - 1)
+
+        return carry
+
+    lax.fori_loop(0, ns + 2 * levels + 1, pipeline, 0)
 
     for b in range(ratio):
         for h in range(nh):
-            @pl.when(jnp.logical_or(ratio * head + b != seq, head != h))
+            off = sum(((h >> level) & 1) * sizes[level] for level in range(1, levels))
+            col = b * 2 * half + (h & 1) * half
+
+            @pl.when(head // 2 == h // 2)
+            def _():
+                out_ref[off : off + sizes[-1], col : col + half] = middle[ratio * head + b, h % 2]
+
+            @pl.when(head // 2 != h // 2)
             def _():
                 pltpu.make_async_remote_copy(
-                    src_ref=fin.at[0], dst_ref=pieces.at[b, h],
-                    send_sem=f_ss.at[0], recv_sem=f_rs.at[b, h],
+                    src_ref=middle.at[0, 0], dst_ref=pieces.at[b, h],
+                    send_sem=p_ss.at[0, 0], recv_sem=p_rs.at[b, h],
                     device_id=(across, head), device_id_type=MESH,
                 ).wait_recv()
-
-            off = sum(((h >> level) & 1) * sizes[level] for level in range(1, levels))
-            col = b * 2 * half + (h & 1) * half
-            out_ref[off : off + sizes[-1], col : col + half] = pieces[b, h]
+                out_ref[off : off + sizes[-1], col : col + half] = pieces[b, h]
 
     def finish(s, carry):
         @pl.when(jnp.logical_and(s % 2 == side, s != seq))
         def _():
             kv_copy(s, chain, (across, head)).wait_send()
             a_copy(s, chain, (across, head)).wait_send()
+
+            @pl.when(forwards(s))
+            def _():
+                to_own_half(s, wait_send)
 
         kv_copy(s, chain + 1, (seq, mate)).wait_send()
         for level in range(levels):
@@ -378,11 +459,16 @@
         def _():
             final_copy(s).wait_send()
 
+        @pl.when(passes(s))
+        def _():
+            for c in range(2):
+                last_copy(s, c).wait_send()
+
         return carry
 
     lax.fori_loop(0, ns, finish, 0)
     spread(kv_copy, wait_send)
-    spread(a_copy, wait_send)
+    spread_attended(wait_send)
 
 
 def local(queries, vision, kv_weight, out_weight, q_gain, k_gain, tile_counts, spans):
@@ -427,9 +513,11 @@
             halved,
             list(halved),
             pltpu.VMEM((ns, last, half), bf16),
+            pltpu.VMEM((ns, 2, last, half), bf16),
             pltpu.VMEM((ns // nh, nh, last, half), bf16),
             dma, dma, dma((ns, ns // 2 + 2)), dma((2, ns)), dma((ns, ns // 2 + 1)), dma((ns,)),
-            dma((levels, ns)), dma((levels, ns)), dma((ns,)), dma((ns // nh, nh)),
+            dma((levels, ns)), dma((levels, ns)), dma((ns,)), dma((ns, 2)), dma((ns, 2)),
+            dma((ns // nh, nh)),
         ],
         compiler_params=pltpu.CompilerParams(
             collective_id=0, has_side_effects=True, vmem_limit_bytes=60 * 2**20

time: 59.6 us -> 63.5 us (1.065)
  the two profiles are of different devices: /device:TPU:25 before, /device:TPU:12 now
where the time goes in v3:
time: 63.5 us; the launch traced here: 63.3 us
  Pallas kernels  61.4 us (97%)
  local copies, waits for them, and re-layouts  1.88 us (3%)
    pallas_call x1, Pallas kernels, local(): pl.pallas_call(functools.partial(kernel, ns, nh), out_shape=jax.ShapeDtyp...  61.4 us
    unnamed x1, local copies, waits for them, and re-layouts  1.88 us

profile of v3, /device:TPU:12, one launch (start us, length us, event | category | flops | bytes accessed | tf_op | source)
XLA Modules:
  0.0 63.3 jit_solution(11367875898822647493)
XLA Ops:
  0.0 61.4 %shard_map.82 = bf16[128,2048]{1,0:T(8,128)(2,1)} custom-call(bf16[128,512]{1,0:T(8,128)(2,1)} %q_hbm.1, bf16[200,8192]{1,0:T(8,128)(2,1)} %x_hbm.1, bf16[128,8192]{1,0:T(8,128)(2,1)} %bitcast.6, bf16[512,1024]{1,0:T(8,128)(2,1)} %ow_hbm.1, f32[1,128]{1,0:T(1,128)} %bitcast.8, f32[1,128]{1,0:T(1,128)} %bitcast.9, s32[4]{0:T(128)} %cnt_hbm.1, s32[2,128]{1,0:T(2,128)} %bitcast.7), custom_call_target="tpu_custom_call" | custom-call | tf_op jit(solution)/shard_map/pallas_call | solution.py:488
  61.4 1.9 %copy.10 = bf16[128,2048]{1,0:T(8,128)(2,1)} copy(bf16[128,2048]{1,0:T(8,128)(2,1)} %shard_map.82) | data formatting | bytes 1048576

commit v4 on v2

--- a/solution.py
+++ b/solution.py
@@ -14,7 +14,7 @@
 MESH = pl.DeviceIdType.MESH
 NT = (((1,), (1,)), ((), ()))
 NN = (((1,), (0,)), ((), ()))
-CHUNK = 1024
+CHUNK = 2048
 
 
 def dot(x, y, dims=NN):
@@ -137,12 +137,15 @@
     block = jnp.where(core == 0, pltpu.roll(block, HD // 2, 1), block)
     kv[core, seq] = block.astype(jnp.bfloat16)
 
+    mid = chain // 2
+    low_half = place < mid
+    base_here = jnp.where(low_half, 0, mid)
+
     def nearest(i):
-        both = jnp.minimum(place, chain - 1 - place)
-        t = (i + 1) // 2
-        near = jnp.where(i % 2 == 1, place - t, place + t)
-        far = jnp.where(place < chain - 1 - place, place + (i - both), place - (i - both))
-        return jnp.where(i <= 2 * both, near, far)
+        crossed = jnp.where(low_half, mid + i - 1, mid - i)
+        rest = base_here + (i - mid - 1)
+        rest = jnp.where(rest >= place, rest + 1, rest)
+        return jnp.where(i == 0, place, jnp.where(i <= mid, crossed, rest))
 
     def kv_copy(s, kind, target):
         return pltpu.make_async_remote_copy(

time: 59.6 us -> 61.9 us (1.039)
  the two profiles are of different devices: /device:TPU:25 before, /device:TPU:3 now
where the time goes in v4:
time: 61.9 us; the launch traced here: 61.2 us
  Pallas kernels  59.3 us (96%)
  local copies, waits for them, and re-layouts  1.88 us (3%)
    pallas_call x1, Pallas kernels, local(): pl.pallas_call(functools.partial(kernel, ns, nh), out_shape=jax.ShapeDtyp...  59.3 us
    unnamed x1, local copies, waits for them, and re-layouts  1.88 us

profile of v4, /device:TPU:3, one launch (start us, length us, event | category | flops | bytes accessed | tf_op | source)
XLA Modules:
  0.0 61.2 jit_solution(2024439499814490888)
XLA Ops:
  0.0 59.3 %shard_map.82 = bf16[128,2048]{1,0:T(8,128)(2,1)} custom-call(bf16[128,512]{1,0:T(8,128)(2,1)} %q_hbm.1, bf16[200,8192]{1,0:T(8,128)(2,1)} %x_hbm.1, bf16[128,8192]{1,0:T(8,128)(2,1)} %bitcast.6, bf16[512,1024]{1,0:T(8,128)(2,1)} %ow_hbm.1, f32[1,128]{1,0:T(1,128)} %bitcast.8, f32[1,128]{1,0:T(1,128)} %bitcast.9, s32[4]{0:T(128)} %cnt_hbm.1, s32[2,128]{1,0:T(2,128)} %bitcast.7), custom_call_target="tpu_custom_call" | custom-call | tf_op jit(solution)/shard_map/pallas_call | solution.py:405
  59.3 1.9 %copy.10 = bf16[128,2048]{1,0:T(8,128)(2,1)} copy(bf16[128,2048]{1,0:T(8,128)(2,1)} %shard_map.82) | data formatting | bytes 1048576

commit v5 on v2

--- a/solution.py
+++ b/solution.py
@@ -140,7 +140,8 @@
     def nearest(i):
         both = jnp.minimum(place, chain - 1 - place)
         t = (i + 1) // 2
-        near = jnp.where(i % 2 == 1, place - t, place + t)
+        inward = jnp.where(place < chain // 2, 1, -1)
+        near = jnp.where(i % 2 == 1, place + inward * t, place - inward * t)
         far = jnp.where(place < chain - 1 - place, place + (i - both), place - (i - both))
         return jnp.where(i <= 2 * both, near, far)
 
@@ -282,13 +283,9 @@
     def first_stage(i):
         s, own_side = turn(i)
 
-        @pl.when(i > 0)
+        @pl.when(jnp.logical_not(own_side))
         def _():
             a_copy(s, chain, (across, head)).wait_recv()
-
-        @pl.when(jnp.logical_and(own_side, i > 0))
-        def _():
-            a_copy(s, chain, (across, head)).start()
 
         rows_in = att[s]
         other = pl.ds(pl.multiple_of((1 - core) * half, half), half)
@@ -296,6 +293,11 @@
         level_copy(0, s).start()
         mine = pl.ds(pl.multiple_of(core * half, half), half)
         keep[s] = dot(rows_in, ow_ref[:, mine])
+
+    def forward(k):
+        s = 2 * nearest(k) + side
+        a_copy(s, chain, (across, head)).wait_recv()
+        a_copy(s, chain, (across, head)).start()
 
     def later_stage(level, i):
         s, _ = turn(i)
@@ -330,10 +332,15 @@
         @pl.when(i == 1)
         def _():
             later_stage(1, 0)
+            forward(1)
 
         @pl.when(i < ns)
         def _():
             first_stage(i)
+
+        @pl.when(jnp.logical_and(i % 2 == 0, jnp.logical_and(i >= 2, i < ns - 2)))
+        def _():
+            forward(i // 2 + 1)
 
         @pl.when(jnp.logical_and(i >= 2, i - 1 < ns))
         def _():

time: 59.6 us -> 61.9 us (1.039)
  Pallas kernels: 57.5 us -> 59.9 us
    pallas_call x1, Pallas kernels: 57.5 us -> 59.9 us  [local(): pl.pallas_call(functools.partial(kernel, ns, nh), out_shape=jax.ShapeDtyp...]
where the time goes in v5:
time: 61.9 us; the launch traced here: 61.8 us
  Pallas kernels  59.9 us (97%)
  local copies, waits for them, and re-layouts  1.88 us (3%)
    pallas_call x1, Pallas kernels, local(): pl.pallas_call(functools.partial(kernel, ns, nh), out_shape=jax.ShapeDtyp...  59.9 us
    unnamed x1, local copies, waits for them, and re-layouts  1.88 us

profile of v5, /device:TPU:25, one launch (start us, length us, event | category | flops | bytes accessed | tf_op | source)
XLA Modules:
  0.0 61.8 jit_solution(12155865496538900428)
XLA Ops:
  0.0 59.9 %shard_map.82 = bf16[128,2048]{1,0:T(8,128)(2,1)} custom-call(bf16[128,512]{1,0:T(8,128)(2,1)} %q_hbm.1, bf16[200,8192]{1,0:T(8,128)(2,1)} %x_hbm.1, bf16[128,8192]{1,0:T(8,128)(2,1)} %bitcast.6, bf16[512,1024]{1,0:T(8,128)(2,1)} %ow_hbm.1, f32[1,128]{1,0:T(1,128)} %bitcast.8, f32[1,128]{1,0:T(1,128)} %bitcast.9, s32[4]{0:T(128)} %cnt_hbm.1, s32[2,128]{1,0:T(2,128)} %bitcast.7), custom_call_target="tpu_custom_call" | custom-call | tf_op jit(solution)/shard_map/pallas_call | solution.py:409
  59.9 1.9 %copy.10 = bf16[128,2048]{1,0:T(8,128)(2,1)} copy(bf16[128,2048]{1,0:T(8,128)(2,1)} %shard_map.82) | data formatting | bytes 1048576

commit v6 on v2

--- a/solution.py
+++ b/solution.py
@@ -126,6 +126,7 @@
         field = q_ref[:, h * HD : (h + 1) * HD].astype(jnp.float32)
         mean_sq = jnp.mean(field * field, axis=1, keepdims=True)
         normed = field / jnp.sqrt(mean_sq + EPSILON) * qg_ref[...]
+        normed = normed * (math.log2(math.e) / math.sqrt(HD))
         swapped = pltpu.roll(normed, HD // 2, 1)
         left_half.append(jnp.where(low, 0.0, swapped).astype(jnp.bfloat16))
         right_half.append(jnp.where(low, swapped, 0.0).astype(jnp.bfloat16))
@@ -140,7 +141,8 @@
     def nearest(i):
         both = jnp.minimum(place, chain - 1 - place)
         t = (i + 1) // 2
-        near = jnp.where(i % 2 == 1, place - t, place + t)
+        outward = jnp.where(place < chain // 2, -1, 1)
+        near = jnp.where(i % 2 == 1, place + outward * t, place - outward * t)
         far = jnp.where(place < chain - 1 - place, place + (i - both), place - (i - both))
         return jnp.where(i <= 2 * both, near, far)
 
@@ -183,7 +185,6 @@
     end = jnp.transpose(jnp.broadcast_to(span_f[1:2, :], (HD, rows)))[:, 0:1]
     first = jnp.concatenate([first] * heads_here, axis=0)
     end = jnp.concatenate([end] * heads_here, axis=0)
-    scale = math.log2(math.e) / math.sqrt(HD)
     numer[...] = jnp.zeros_like(numer)
     wsum[...] = jnp.zeros_like(wsum)
 
@@ -204,7 +205,7 @@
         tile = jnp.where(present, tile, 2 * TILES).astype(jnp.float32)
         allowed = jnp.logical_and(first <= tile, tile < end)
         both = jnp.concatenate([kv[0, s], kv[1, s]], axis=1)
-        weights = jnp.where(allowed, jnp.exp2(dot(slots, both, NT) * scale), 0.0)
+        weights = jnp.where(allowed, jnp.exp2(dot(slots, both, NT)), 0.0)
         wsum[...] += weights
         numer[...] += dot(weights.astype(jnp.bfloat16), both)
 

time: 59.6 us -> 60.5 us (1.015)
  the two profiles are of different devices: /device:TPU:25 before, /device:TPU:3 now
where the time goes in v6:
time: 60.5 us; the launch traced here: 60.4 us
  Pallas kernels  58.5 us (97%)
  local copies, waits for them, and re-layouts  1.88 us (3%)
    pallas_call x1, Pallas kernels, local(): pl.pallas_call(functools.partial(kernel, ns, nh), out_shape=jax.ShapeDtyp...  58.5 us
    unnamed x1, local copies, waits for them, and re-layouts  1.88 us

profile of v6, /device:TPU:3, one launch (start us, length us, event | category | flops | bytes accessed | tf_op | source)
XLA Modules:
  0.0 60.4 jit_solution(4357002086273212341)
XLA Ops:
  0.0 58.5 %shard_map.82 = bf16[128,2048]{1,0:T(8,128)(2,1)} custom-call(bf16[128,512]{1,0:T(8,128)(2,1)} %q_hbm.1, bf16[200,8192]{1,0:T(8,128)(2,1)} %x_hbm.1, bf16[128,8192]{1,0:T(8,128)(2,1)} %bitcast.6, bf16[512,1024]{1,0:T(8,128)(2,1)} %ow_hbm.1, f32[1,128]{1,0:T(1,128)} %bitcast.8, f32[1,128]{1,0:T(1,128)} %bitcast.9, s32[4]{0:T(128)} %cnt_hbm.1, s32[2,128]{1,0:T(2,128)} %bitcast.7), custom_call_target="tpu_custom_call" | custom-call | tf_op jit(solution)/shard_map/pallas_call | solution.py:403
  58.5 1.9 %copy.10 = bf16[128,2048]{1,0:T(8,128)(2,1)} copy(bf16[128,2048]{1,0:T(8,128)(2,1)} %shard_map.82) | data formatting | bytes 1048576

commit v7 on v5

--- a/solution.py
+++ b/solution.py
@@ -14,7 +14,7 @@
 MESH = pl.DeviceIdType.MESH
 NT = (((1,), (1,)), ((), ()))
 NN = (((1,), (0,)), ((), ()))
-CHUNK = 1024
+CHUNK = 2048
 
 
 def dot(x, y, dims=NN):
@@ -140,8 +140,7 @@
     def nearest(i):
         both = jnp.minimum(place, chain - 1 - place)
         t = (i + 1) // 2
-        inward = jnp.where(place < chain // 2, 1, -1)
-        near = jnp.where(i % 2 == 1, place + inward * t, place - inward * t)
+        near = jnp.where(i % 2 == 1, place - t, place + t)
         far = jnp.where(place < chain - 1 - place, place + (i - both), place - (i - both))
         return jnp.where(i <= 2 * both, near, far)
 

time: 61.9 us -> 58.8 us (0.950)
  the two profiles are of different devices: /device:TPU:25 before, /device:TPU:3 now
where the time goes in v7:
time: 58.8 us; the launch traced here: 58.6 us
  Pallas kernels  56.7 us (96%)
  local copies, waits for them, and re-layouts  1.88 us (3%)
    pallas_call x1, Pallas kernels, local(): pl.pallas_call(functools.partial(kernel, ns, nh), out_shape=jax.ShapeDtyp...  56.7 us
    unnamed x1, local copies, waits for them, and re-layouts  1.88 us

profile of v7, /device:TPU:3, one launch (start us, length us, event | category | flops | bytes accessed | tf_op | source)
XLA Modules:
  0.0 58.6 jit_solution(9817102055671811868)
XLA Ops:
  0.0 56.7 %shard_map.82 = bf16[128,2048]{1,0:T(8,128)(2,1)} custom-call(bf16[128,512]{1,0:T(8,128)(2,1)} %q_hbm.1, bf16[200,8192]{1,0:T(8,128)(2,1)} %x_hbm.1, bf16[128,8192]{1,0:T(8,128)(2,1)} %bitcast.6, bf16[512,1024]{1,0:T(8,128)(2,1)} %ow_hbm.1, f32[1,128]{1,0:T(1,128)} %bitcast.8, f32[1,128]{1,0:T(1,128)} %bitcast.9, s32[4]{0:T(128)} %cnt_hbm.1, s32[2,128]{1,0:T(2,128)} %bitcast.7), custom_call_target="tpu_custom_call" | custom-call | tf_op jit(solution)/shard_map/pallas_call | solution.py:408
  56.7 1.9 %copy.10 = bf16[128,2048]{1,0:T(8,128)(2,1)} copy(bf16[128,2048]{1,0:T(8,128)(2,1)} %shard_map.82) | data formatting | bytes 1048576
